TPU v7x, 32 devices: a whole 2x2x4 slice. The times are simulated.
32 devices in a mesh: ens: 2 (over x), cells: 16 (over z, y, core).
Axes of the slice: x: 2, y: 2, z: 4, core: 2. Of those that a mesh axis runs over, the one named last changes fastest.
Arguments:
- control: float32 [64, 128, 2048], P('ens', 'cells'), parts along dimension 0
- prior_flux: float32 [32, 128, 2048], P(None, 'cells'), may hold values from -6 to 6
- area_weight: float32 [128, 2048], P('cells')
- time_factor: float32 [32, 32], replicated
- lat_factor: float32 [128, 128], replicated
- coarse_lon: float32 [16, 16], replicated
- fine_lon: float32 [128, 128], replicated
- footprint_tiles: int32 [2048, 8], P('cells'), may hold values from 0 to 2047, as said below
- footprint_hours: int32 [2048, 8], P('cells'), may hold values from 0 to 31
- footprint_weights: bfloat16 [2048, 8, 128], P('cells'), may hold values from -0.09472656 to 0.10498047
- observations: float32 [4096], P(('ens', 'cells')), parts along dimension 0, may hold values from -4 to 0
- error_variance: float32 [2048], P('cells'), may hold values from 0.5 to 4
Outputs:
- gradient: float32 [64, 128, 2048], P('ens', 'cells'), parts along dimension 0
- misfit: float32 [4096], P(('ens', 'cells')), parts along dimension 0
There are 2 independent parts, one for each index of `ens`. A program takes and returns all parts, laid end to end along the dimension named above; an argument that names none is the same for every part. Nothing has to cross between parts.
Inputs may be any that keep to these rules, and one draw needn't show every extreme that they name: A tile's cells belong to device footprint_tiles // 128. The slots of one device's soundings name tiles of any one device at most 128 times, and exactly 128 times for some device.
All inputs are finite; a program needn't handle non-finite values.
Results may differ from a plain program's by a relative error of at most 0.0021.
Values may be sent and summed in bfloat16 or wider, within the bound.
A program may use at most 128 MiB of HBM per device.

v0:
```python
import functools

import jax
import jax.numpy as jnp
from jax import lax
from jax.experimental import pallas as pl
from jax.experimental.pallas import tpu as pltpu
from jax.sharding import PartitionSpec as P

highest = lax.Precision.HIGHEST


def lon_apply(field, coarse_lon, fine_lon):
    shaped = field.reshape(field.shape[0], field.shape[1], coarse_lon.shape[0], fine_lon.shape[0])
    shaped = jnp.einsum("hapq,fq->hapf", shaped, fine_lon, precision=highest)
    shaped = jnp.einsum("hapf,cp->hacf", shaped, coarse_lon, precision=highest)
    return shaped.reshape(field.shape)


def lon_adjoint(field, coarse_lon, fine_lon):
    shaped = field.reshape(field.shape[0], field.shape[1], coarse_lon.shape[0], fine_lon.shape[0])
    shaped = jnp.einsum("hapq,qf->hapf", shaped, fine_lon, precision=highest)
    shaped = jnp.einsum("hapf,pc->hacf", shaped, coarse_lon, precision=highest)
    return shaped.reshape(field.shape)


def time_apply(field, time_factor):
    return jnp.einsum("gh,hab->gab", time_factor, field, precision=highest)


def time_adjoint(field, time_factor):
    return jnp.einsum("hg,hab->gab", time_factor, field, precision=highest)


def lat_apply(field, lat_factor):
    return jnp.einsum("ca,hab->hcb", lat_factor, field, precision=highest)


def lat_adjoint(field, lat_factor):
    return jnp.einsum("ac,hab->hcb", lat_factor, field, precision=highest)


def to_columns(field):
    return lax.all_to_all(field, "cells", split_axis=2, concat_axis=1, tiled=True)


def to_rows(field):
    return lax.all_to_all(field, "cells", split_axis=1, concat_axis=2, tiled=True)


def by_latitude(
    control,
    prior_flux,
    area_weight,
    time_factor,
    lat_factor,
    coarse_lon,
    fine_lon,
    footprint_tiles,
    footprint_hours,
    footprint_weights,
    observations,
    error_variance,
):
    devices = lax.axis_size("cells")
    hours_count = control.shape[0]
    tile_width = footprint_weights.shape[2]
    spread = lon_apply(control, coarse_lon, fine_lon)
    spread = time_apply(spread, time_factor)
    increment = to_rows(lat_apply(to_columns(spread), lat_factor))
    hourly, total_weight = lax.psum(
        (jnp.sum(increment, axis=(1, 2)), jnp.sum(area_weight)), "cells"
    )
    flux_field = prior_flux + increment - area_weight[None] * (hourly / total_weight)[:, None, None]
    flux_rows = flux_field.astype(jnp.bfloat16).reshape(-1, tile_width)
    tile_count = flux_rows.shape[0] // hours_count
    slot_total = footprint_tiles.size
    capacity = 2 * slot_total // devices
    owners = (footprint_tiles // tile_count).reshape(-1)
    row_index = (footprint_hours * tile_count + footprint_tiles % tile_count).reshape(-1)
    order = jnp.argsort(owners, stable=True)
    sorted_owners = owners[order]
    starts = jnp.searchsorted(sorted_owners, jnp.arange(devices, dtype=jnp.int32))
    ranked = jnp.arange(slot_total, dtype=jnp.int32) - starts[sorted_owners]
    target = jnp.zeros((slot_total,), jnp.int32).at[order].set(sorted_owners * capacity + ranked)
    weights_flat = footprint_weights.reshape(slot_total, tile_width)
    request_rows = (
        jnp.zeros((devices * capacity,), jnp.int32)
        .at[target]
        .set(row_index)
        .reshape(devices, capacity)
    )
    send_weights = (
        jnp.zeros((devices * capacity, tile_width), jnp.bfloat16).at[target].set(weights_flat)
    )
    got_weights, got_rows = (
        lax.all_to_all(
            send_weights.reshape(devices, capacity, tile_width),
            "cells",
            split_axis=0,
            concat_axis=0,
            tiled=True,
        ),
        lax.all_to_all(request_rows, "cells", split_axis=0, concat_axis=0, tiled=True),
    )
    got_index = got_rows.reshape(-1)
    got_flat = got_weights.reshape(-1, tile_width)
    shares = jnp.einsum(
        "sc,sc->s", flux_rows[got_index], got_flat, preferred_element_type=jnp.float32
    )
    returned = lax.all_to_all(
        shares.reshape(devices, capacity), "cells", split_axis=0, concat_axis=0, tiled=True
    )
    predicted = returned.reshape(-1)[target].reshape(footprint_tiles.shape).sum(axis=1)
    misfit = (predicted - observations) / error_variance
    slot_misfit = jnp.broadcast_to(misfit[:, None], footprint_tiles.shape).reshape(-1)
    send_misfit = jnp.zeros((devices * capacity,), jnp.float32).at[target].set(slot_misfit)
    got_misfit = lax.all_to_all(
        send_misfit.reshape(devices, capacity), "cells", split_axis=0, concat_axis=0, tiled=True
    )
    contrib = got_flat * got_misfit.reshape(-1)[:, None]
    grad_rows = jnp.zeros(flux_rows.shape, jnp.float32).at[got_index].add(contrib)
    grad_flux = grad_rows.reshape(prior_flux.shape)
    weighted = lax.psum(jnp.sum(area_weight[None] * grad_flux, axis=(1, 2)), "cells")
    projected = grad_flux - (weighted / total_weight)[:, None, None]
    back = to_rows(lat_adjoint(to_columns(projected), lat_factor))
    back = time_adjoint(back, time_factor)
    back = lon_adjoint(back, coarse_lon, fine_lon)
    return (control + back, misfit)


MESH_BUDGET = 56 * 1024 * 1024
LANES = 128
SUB = 8


def dot(left, right, left_dim, right_dim):
    return lax.dot_general(
        left,
        right,
        (((left_dim,), (right_dim,)), ((), ())),
        precision=highest,
        preferred_element_type=jnp.float32,
    )


def iota(shape, dim):
    return lax.broadcasted_iota(jnp.int32, shape, dim)


def spread_matrix(factor, repeat, adjoint):
    size = factor.shape[0]
    pick = (iota((size * repeat, size), 0) // repeat == iota((size * repeat, size), 1)).astype(jnp.float32)
    wide = dot(dot(pick, factor, 1, 1 if adjoint else 0), pick, 1, 1)
    whole = (size * repeat, size * repeat)
    return jnp.where(iota(whole, 0) % repeat == iota(whole, 1) % repeat, wide, 0.0)


def encode(blocks, scales, at, out_ref, column):
    largest = jnp.maximum(jnp.max(jnp.abs(blocks), axis=(1, 2), keepdims=True), 1e-33)
    out_ref[:, at, :] = jnp.round(blocks * (32767.0 / largest)).astype(jnp.int32).astype(jnp.int16)
    return jnp.where(iota(scales.shape, 2) == column, largest * (1.0 / 32767.0), scales)


def decode(coded, steps, chunk):
    rows = coded.shape[0]
    pick = (iota((rows, LANES), 1) == iota((rows, LANES), 0) // chunk).astype(jnp.float32)
    return coded.astype(jnp.int32).astype(jnp.float32) * dot(pick, jnp.broadcast_to(steps, (LANES, LANES)), 1, 1)


def split(value, size):
    if size & (size - 1) == 0:
        return lax.shift_right_logical(value, size.bit_length() - 1), value & (size - 1)
    return lax.div(value, size), lax.rem(value, size)


def greet(devices, me):
    barrier = pltpu.get_barrier_semaphore()
    for step in range(1, devices):
        pl.semaphore_signal(
            barrier, inc=1, device_id={"cells": lax.rem(me + step, devices)}, device_id_type=pl.DeviceIdType.MESH
        )
    pl.semaphore_wait(barrier, devices - 1)


def send_to(devices, me, step, source, target, send_sem, recv_sem):
    return pltpu.make_async_remote_copy(
        src_ref=source,
        dst_ref=target,
        send_sem=send_sem,
        recv_sem=recv_sem,
        device_id={"cells": lax.rem(me + step, devices)},
        device_id_type=pl.DeviceIdType.MESH,
    )


def forward_kernel(
    devices, x_ref, area_ref, time_ref, lat_ref, coarse_ref, fine_ref,
    inc_ref, area_out, totals_ref,
    work, sums, sendb, recvb, small_out, small_in, send_sem, recv_sem, small_send, small_recv,
):
    me = lax.axis_index("cells")
    rows = x_ref.shape[0]
    hours = time_ref.shape[0]
    chunk = rows // devices
    time_wide = spread_matrix(time_ref[...], SUB, False)
    coarse_wide = spread_matrix(coarse_ref[...], chunk, False)

    def fine_step(p, carry):
        part = x_ref[:, pl.ds(pl.multiple_of(p * LANES, LANES), LANES)]
        work[p] = dot(dot(time_wide, part, 1, 0), fine_ref[...], 1, 1)
        return carry

    lax.fori_loop(0, devices, fine_step, 0)

    def coarse_step(r, carry):
        at = pl.ds(pl.multiple_of(r * chunk, chunk), chunk)
        mixed = dot(coarse_wide, work[:, at, :].reshape(devices * chunk, LANES), 1, 0).reshape(devices, chunk, LANES)
        sums[at, :] = jnp.sum(mixed, axis=0)
        return encode(mixed, carry, at, sendb, r)

    scales = lax.fori_loop(0, devices, coarse_step, jnp.zeros((devices, SUB, LANES), jnp.float32))
    greet(devices, me)
    copies = []
    for step in range(1, devices):
        peer = lax.rem(me + step, devices)
        copies.append(send_to(devices, me, step, sendb.at[peer], recvb.at[me], send_sem.at[step], recv_sem.at[step]))
        copies[-1].start()

    ones = jnp.ones((SUB, LANES), jnp.float32)
    lat_sums = dot(ones, lat_ref[...], 1, 0)
    place = (iota((LANES, rows), 0) == SUB * me + iota((LANES, rows), 1) % SUB).astype(jnp.float32)
    lat_row = dot(lat_sums, place, 1, 0)[0:1]
    hour_weights = jnp.where(iota((LANES, rows), 0) == iota((LANES, rows), 1) // SUB, lat_row, 0.0)
    mine = dot(ones, dot(hour_weights, sums[...], 1, 0), 1, 1)
    area_total = jnp.sum(jnp.sum(area_ref[...], axis=1, keepdims=True), axis=0, keepdims=True)
    mine = jnp.where(iota((SUB, LANES), 1) == hours, area_total, mine)
    for p in range(devices):
        small_out[p, 0:SUB] = area_ref[:, p * LANES:(p + 1) * LANES]
        small_out[p, SUB:2 * SUB] = jnp.where(iota((SUB, LANES), 0) < SUB // 2, mine, scales[p])
    for step in range(1, devices):
        peer = lax.rem(me + step, devices)
        copies.append(
            send_to(devices, me, step, small_out.at[peer], small_in.at[me], small_send.at[step], small_recv.at[step])
        )
        copies[-1].start()
    recvb[me] = sendb[me]
    small_in[me] = small_out[me]
    for copy in copies:
        copy.wait()
    total = small_in[0, SUB:SUB + 1]
    for p in range(1, devices):
        total = total + small_in[p, SUB:SUB + 1]
    total = jnp.broadcast_to(total, (SUB, LANES))
    weight = total[:, hours:hours + 1]
    totals_ref[...] = jnp.where(iota((SUB, LANES), 1) == hours, total, total / weight)
    for p in range(devices):
        area_out[SUB * p:SUB * (p + 1), :] = small_in[p, 0:SUB]
        work[p] = decode(recvb[p], small_in[p, 2 * SUB - 1:2 * SUB], chunk)
    lat = lat_ref[...]

    def lat_step(h, carry):
        at = pl.ds(pl.multiple_of(h * SUB, SUB), SUB)
        column = work[:, at, :].reshape(devices * SUB, LANES)
        inc_ref[pl.ds(pl.multiple_of(h * LANES, LANES), LANES), :] = dot(lat, column, 1, 0)
        return carry

    lax.fori_loop(0, hours, lat_step, 0, unroll=4)


def share_kernel(
    devices, slots, foot, lists, mean, weights_ref, inc_ref, prior_ref, area_ref, out_ref, wide, prior_rows, shares
):
    me = lax.axis_index("cells")
    rows = prior_ref.shape[0]
    soundings = slots // foot
    stride = lists.shape[0] // (2 * devices)

    def widen(s, carry):
        at = pl.ds(pl.multiple_of(s * slots, slots), slots)
        wide[at, :] = weights_ref[s].astype(jnp.float32)
        shares[at, :] = jnp.zeros((slots, LANES), jnp.float32)
        return carry

    lax.fori_loop(0, devices, widen, 0)

    def prior_step(h, carry):
        level = mean[h]
        for p in range(devices):
            lanes = slice(p * LANES, (p + 1) * LANES)
            prior_rows[pl.ds(pl.multiple_of(p * rows + h * SUB, SUB), SUB), :] = (
                prior_ref[pl.ds(pl.multiple_of(h * SUB, SUB), SUB), lanes] - area_ref[:, lanes] * level
            )
        return carry

    lax.fori_loop(0, rows // SUB, prior_step, 0)

    def each_source(which, table, add):
        def source(s, carry):
            base = (2 * s + which) * stride
            low = lists[base + slots + me]
            high = lists[base + slots + me + 1]

            def group(first, count):
                products, places = [], []
                for j in range(count):
                    value = lists[base + first + j]
                    row, slot = split(value, slots)
                    row = split(row, table.shape[0])[1]
                    sounding, k = split(slot, foot)
                    place = k * (devices * soundings) + s * soundings + sounding
                    product = table[pl.ds(row, 1), :] * wide[pl.ds(s * slots + slot, 1), :]
                    if add:
                        product = product + shares[pl.ds(place, 1), :]
                    products.append(product)
                    places.append(place)
                for place, product in zip(places, products):
                    shares[pl.ds(place, 1), :] = product

            groups = (high - low) // 8

            def full(i, inner):
                group(low + i * 8, 8)
                return inner

            def rest(i, inner):
                group(i, 1)
                return inner

            lax.fori_loop(0, groups, full, 0)
            lax.fori_loop(low + groups * 8, high, rest, 0)
            return carry

        lax.fori_loop(0, devices, source, 0)

    each_source(0, inc_ref, False)
    each_source(1, prior_rows, True)
    ones = jnp.ones((SUB, LANES), jnp.float32)

    def collect(s, carry):
        summed = shares[pl.ds(pl.multiple_of(s * soundings, soundings), soundings), :]
        for k in range(1, foot):
            at = pl.multiple_of(k * devices * soundings + s * soundings, soundings)
            summed = summed + shares[pl.ds(at, soundings), :]
        out_ref[s] = dot(ones, summed, 1, 1)
        return carry

    lax.fori_loop(0, devices, collect, 0)


def misfit_kernel(
    devices, part_ref, seen_ref, variance_ref, all_ref, own_ref,
    got, spread, mine, send_sem, recv_sem, back_send, back_recv,
):
    me = lax.axis_index("cells")
    greet(devices, me)
    copies = []
    for step in range(1, devices):
        peer = lax.rem(me + step, devices)
        copies.append(send_to(devices, me, step, part_ref.at[peer], got.at[me], send_sem.at[step], recv_sem.at[step]))
        copies[-1].start()
    got[me] = part_ref[me]
    for copy in copies:
        copy.wait()
    predicted = got[0]
    for p in range(1, devices):
        predicted = predicted + got[p]
    misfit = (predicted - seen_ref[...]) / variance_ref[...]
    mine[...] = misfit
    copies = []
    for step in range(1, devices):
        copies.append(send_to(devices, me, step, mine, spread.at[me], back_send.at[step], back_recv.at[step]))
        copies[-1].start()
    spread[me] = misfit
    own_ref[...] = misfit
    for copy in copies:
        copy.wait()
    all_ref[...] = spread[...]


def scatter_kernel(devices, slots, foot, lists, misfit, weights_ref, grad_ref, wide):
    me = lax.axis_index("cells")
    soundings = slots // foot
    stride = lists.shape[0] // (2 * devices)
    cells = grad_ref.shape[0]

    def widen(s, carry):
        at = pl.ds(pl.multiple_of(s * slots, slots), slots)
        wide[at, :] = weights_ref[s].astype(jnp.float32)
        part = cells // devices
        grad_ref[pl.ds(pl.multiple_of(s * part, part), part), :] = jnp.zeros((part, LANES), jnp.float32)
        return carry

    lax.fori_loop(0, devices, widen, 0)

    def source(s, carry):
        base = 2 * s * stride
        low = lists[base + slots + me]
        high = lists[base + slots + me + 1]

        def group(first, count):
            products, places = [], []
            for j in range(count):
                value = lists[base + first + j]
                row, slot = split(value, slots)
                places.append(split(row, cells)[1])
                products.append(wide[pl.ds(s * slots + slot, 1), :] * misfit[s * soundings + split(slot, foot)[0]])
            for place, product in zip(places, products):
                grad_ref[pl.ds(place, 1), :] += product

        groups = (high - low) // 8

        def full(i, inner):
            group(low + i * 8, 8)
            return inner

        def rest(i, inner):
            group(i, 1)
            return inner

        lax.fori_loop(0, groups, full, 0)
        lax.fori_loop(low + groups * 8, high, rest, 0)
        return carry

    lax.fori_loop(0, devices, source, 0)


def adjoint_kernel(
    devices, grad_ref, area_ref, totals_ref, x_ref, time_ref, lat_ref, coarse_ref, fine_ref, out_ref,
    work, mixed, hour_sums, sendb, recvb, small_out, small_in, send_sem, recv_sem, small_send, small_recv,
):
    me = lax.axis_index("cells")
    rows = x_ref.shape[0]
    hours = time_ref.shape[0]
    chunk = rows // devices
    lat = lat_ref[...].T
    hour_sums[...] = jnp.zeros(hour_sums.shape, jnp.float32)

    def lat_step(h, carry):
        field = grad_ref[pl.ds(pl.multiple_of(h * LANES, LANES), LANES), :]
        at = pl.ds(pl.multiple_of(h * SUB, SUB), SUB)
        work[:, at, :] = dot(lat, field, 1, 0).reshape(devices, SUB, LANES)
        hour_sums[pl.ds(h, 1), :] = jnp.sum(field * area_ref[...], axis=0, keepdims=True)
        return carry

    lax.fori_loop(0, hours, lat_step, 0, unroll=4)

    def encode_step(r, carry):
        at = pl.ds(pl.multiple_of(r * chunk, chunk), chunk)
        return encode(work[:, at, :], carry, at, sendb, r)

    scales = lax.fori_loop(0, devices, encode_step, jnp.zeros((devices, SUB, LANES), jnp.float32))
    greet(devices, me)
    copies = []
    for step in range(1, devices):
        peer = lax.rem(me + step, devices)
        copies.append(send_to(devices, me, step, sendb.at[peer], recvb.at[me], send_sem.at[step], recv_sem.at[step]))
        copies[-1].start()
    ones = jnp.ones((SUB, LANES), jnp.float32)
    weighted = dot(ones, hour_sums[...], 1, 1)
    for p in range(devices):
        small_out[p] = jnp.where(iota((SUB, LANES), 0) < SUB // 2, weighted, scales[p])
    for step in range(1, devices):
        peer = lax.rem(me + step, devices)
        copies.append(
            send_to(devices, me, step, small_out.at[peer], small_in.at[me], small_send.at[step], small_recv.at[step])
        )
        copies[-1].start()
    small_in[me] = small_out[me]
    recvb[me] = sendb[me]
    time_wide = spread_matrix(time_ref[...], SUB, True)
    coarse_wide = spread_matrix(coarse_ref[...], chunk, True)
    square = jnp.ones((LANES, LANES), jnp.float32)
    lat_sums = dot(square, lat_ref[...], 1, 0)
    place = (iota((rows, LANES), 1) == SUB * me + iota((rows, LANES), 0) % SUB).astype(jnp.float32)
    lat_column = dot(place, lat_sums, 1, 1)
    for copy in copies:
        copy.wait()
    total = small_in[0, 0:1]
    for p in range(1, devices):
        total = total + small_in[p, 0:1]
    level = total / totals_ref[0:1, hours:hours + 1]
    hour_of = (iota((rows, LANES), 1) == iota((rows, LANES), 0) // SUB).astype(jnp.float32)
    level_column = dot(hour_of, jnp.broadcast_to(level, (LANES, LANES)), 1, 1)
    shift = lat_column * level_column
    for p in range(devices):
        work[p] = decode(recvb[p], small_in[p, SUB - 1:SUB], chunk) - shift

    def coarse_step(r, carry):
        at = pl.ds(pl.multiple_of(r * chunk, chunk), chunk)
        mixed[:, at, :] = dot(coarse_wide, work[:, at, :].reshape(devices * chunk, LANES), 1, 0).reshape(
            devices, chunk, LANES
        )
        return carry

    lax.fori_loop(0, devices, coarse_step, 0)

    def fine_step(p, carry):
        lanes = pl.ds(pl.multiple_of(p * LANES, LANES), LANES)
        out_ref[:, lanes] = x_ref[:, lanes] + dot(time_wide, dot(mixed[p], fine_ref[...], 1, 0), 1, 0)
        return carry

    lax.fori_loop(0, devices, fine_step, 0)


def f32(*shape):
    return jax.ShapeDtypeStruct(shape, jnp.float32)


def vmem(count):
    return [pl.BlockSpec(memory_space=pltpu.VMEM)] * count


def smem(count):
    return [pl.BlockSpec(memory_space=pltpu.SMEM)] * count


def by_longitude(
    control,
    prior_flux,
    area_weight,
    time_factor,
    lat_factor,
    coarse_lon,
    fine_lon,
    footprint_tiles,
    footprint_hours,
    footprint_weights,
    observations,
    error_variance,
):
    devices = lax.axis_size("cells")
    hours, lat_rows, longitude = control.shape
    latitude = lat_factor.shape[0]
    rows = hours * lat_rows
    foot = footprint_tiles.shape[1]
    slots = footprint_tiles.size
    soundings = footprint_tiles.shape[0]
    cells = hours * latitude

    gathered = lax.all_gather(footprint_weights.reshape(slots, LANES), "cells", axis=0, tiled=False)
    tiles = footprint_tiles.reshape(-1)
    hour = footprint_hours.reshape(-1)
    lat = tiles // devices
    tile = tiles % devices
    slot = jnp.arange(slots, dtype=jnp.int32)
    by_lon = (tile * cells + hour * latitude + lat) * slots + slot
    by_lat = ((lat // lat_rows) * cells + tile * rows + hour * lat_rows + lat % lat_rows) * slots + slot
    ordered = lax.sort(jnp.stack([by_lon, by_lat]), dimension=1)
    edges = jnp.arange(LANES, dtype=jnp.int32) * (cells * slots)
    starts = jnp.sum((ordered[:, None, :] < edges[None, :, None]).astype(jnp.int32), axis=2)
    lists = lax.all_gather(jnp.concatenate([ordered, starts], axis=1).reshape(-1), "cells", axis=0, tiled=True)

    x = control.reshape(rows, longitude)
    prior = prior_flux.reshape(rows, longitude)
    sems = [pltpu.SemaphoreType.DMA((devices,))] * 4
    blocks = (devices, rows, LANES)
    limits = dict(vmem_limit_bytes=MESH_BUDGET, has_side_effects=True)
    increment, area_column, totals = pl.pallas_call(
        functools.partial(forward_kernel, devices),
        out_shape=(f32(cells, LANES), f32(latitude, LANES), f32(SUB, LANES)),
        in_specs=vmem(6),
        out_specs=tuple(vmem(3)),
        scratch_shapes=[
            pltpu.VMEM(blocks, jnp.float32),
            pltpu.VMEM((rows, LANES), jnp.float32),
            pltpu.VMEM(blocks, jnp.int16),
            pltpu.VMEM(blocks, jnp.int16),
            pltpu.VMEM((devices, 2 * SUB, LANES), jnp.float32),
            pltpu.VMEM((devices, 2 * SUB, LANES), jnp.float32),
        ] + sems,
        compiler_params=pltpu.CompilerParams(collective_id=0, **limits),
    )(x, area_weight, time_factor, lat_factor, coarse_lon, fine_lon)

    partial = pl.pallas_call(
        functools.partial(share_kernel, devices, slots, foot),
        out_shape=f32(devices, SUB, soundings),
        in_specs=smem(2) + vmem(4),
        out_specs=vmem(1)[0],
        scratch_shapes=[
            pltpu.VMEM((devices * slots, LANES), jnp.float32),
            pltpu.VMEM((cells, LANES), jnp.float32),
            pltpu.VMEM((devices * slots, LANES), jnp.float32),
        ],
        compiler_params=pltpu.CompilerParams(vmem_limit_bytes=MESH_BUDGET),
    )(lists, totals[0], gathered, increment, prior, area_weight)

    small = pltpu.VMEM((devices, SUB, LANES), jnp.float32)
    every, own = pl.pallas_call(
        functools.partial(misfit_kernel, devices),
        out_shape=(f32(devices, SUB, soundings), f32(SUB, soundings)),
        in_specs=vmem(3),
        out_specs=tuple(vmem(2)),
        scratch_shapes=[small, small, pltpu.VMEM((SUB, LANES), jnp.float32)] + sems,
        compiler_params=pltpu.CompilerParams(collective_id=1, **limits),
    )(partial, observations.reshape(1, soundings), error_variance.reshape(1, soundings))

    grad = pl.pallas_call(
        functools.partial(scatter_kernel, devices, slots, foot),
        out_shape=f32(cells, LANES),
        in_specs=smem(2) + vmem(1),
        out_specs=vmem(1)[0],
        scratch_shapes=[pltpu.VMEM((devices * slots, LANES), jnp.float32)],
        compiler_params=pltpu.CompilerParams(vmem_limit_bytes=MESH_BUDGET),
    )(lists, every[:, 0].reshape(-1), gathered)

    gradient = pl.pallas_call(
        functools.partial(adjoint_kernel, devices),
        out_shape=f32(rows, longitude),
        in_specs=vmem(8),
        out_specs=vmem(1)[0],
        scratch_shapes=[
            pltpu.VMEM(blocks, jnp.float32),
            pltpu.VMEM(blocks, jnp.float32),
            pltpu.VMEM((LANES, LANES), jnp.float32),
            pltpu.VMEM(blocks, jnp.int16),
            pltpu.VMEM(blocks, jnp.int16),
            small,
            small,
        ] + sems,
        compiler_params=pltpu.CompilerParams(collective_id=2, **limits),
    )(grad, area_column, totals, x, time_factor, lat_factor, coarse_lon, fine_lon)
    return gradient.reshape(control.shape), own[0]


def fits(devices, control, coarse_lon, fine_lon, lat_factor, footprint_tiles):
    return (
        devices == coarse_lon.shape[0]
        and fine_lon.shape[0] == LANES
        and control.shape[1] == SUB
        and lat_factor.shape[0] == LANES
        and footprint_tiles.shape[0] == LANES
        and (control.shape[0] * SUB) % (16 * devices) == 0
        and control.shape[0] < LANES
        and devices * control.shape[0] * LANES * footprint_tiles.size < 2**31
        and devices < LANES
    )


def per_device(*arrays):
    devices = lax.axis_size("cells")
    control, lat_factor, coarse_lon, fine_lon, footprint_tiles = (arrays[i] for i in (0, 4, 5, 6, 7))
    if fits(devices, control, coarse_lon, fine_lon, lat_factor, footprint_tiles):
        return by_longitude(*arrays)
    return by_latitude(*arrays)


def solution(mesh):
    placed = (
        P("ens", "cells", None),
        P(None, "cells", None),
        P("cells", None),
        P(),
        P(),
        P(),
        P(),
        P("cells", None),
        P("cells", None),
        P("cells", None, None),
        P(("ens", "cells")),
        P("cells"),
    )
    return jax.shard_map(
        per_device,
        mesh=mesh,
        in_specs=placed,
        out_specs=(P("ens", "cells", None), P(("ens", "cells"))),
        check_vma=False,
    )
```

profile of v0, /device:TPU:0, one launch (start us, length us, event | category | flops | bytes accessed | tf_op | source)
XLA Modules:
  0.0 228.8 jit_solution(8323087858530825477)
XLA Ops:
  8.0 0.0 sort.9.cloned.1.call-start
  8.0 0.7 broadcast_multiply_fusion.1
  8.7 0.1 copy.21
  8.8 0.1 mul.96
  8.9 0.1 copy.22
  9.0 0.1 mul.102
  9.1 0.8 copy.20
  9.9 0.1 reshape.274
  10.1 0.1 iota_add_fusion
  10.1 0.6 pad_add_fusion.1
  10.7 0.0 sort.9.cloned.1.call-update
  10.8 0.0 all-gather.3.cloned.1.call-start
  10.8 0.5 all-gather.3.cloned.1.call-update
  11.3 77.6 %shard_map.131 = (f32[4096,128]{1,0:T(8,128)}, f32[128,128]{1,0:T(8,128)}, f32[8,128]{1,0:T(8,128)}) custom-call(f32[256,2048]{1,0:T(8,128)} %bitcast.12, f32[8,2048]{1,0:T(8,128)} %area_ref.3, f32[32,32]{1,0:T(8,128)} %time_ref.3, f32[128,128]{1,0:T(8,128)} %lat_ref.3, f32[16,16]{1,0:T(8,128)} %coarse_ref.3, f32[128,128]{1,0:T(8,128)} %fine_ref.3), custom_call_target="tpu_custom_call" | custom-call | tf_op jit(solution)/shard_map/pallas_call | solution.py:559
  89.0 1.2 slice_bitcast_fusion.1.mean
  90.2 0.0 sort.9.cloned.1.call-done
  90.2 0.9 convert_reduce_fusion
  91.1 0.7 pad_add_fusion
  91.8 23.0 %all-gather = s32[16,1,2304]{2,1,0:T(1,128)} all-gather(s32[1,1,2304]{2,1,0:T(1,128)S(1)} %reshape.281), channel_id=1, replica_groups=mesh['ens'=2,'cells'=16] {'cells'}, dimensions={0}, use_global_device_ids=true | all-gather | bytes 156672 | tf_op jit(solution)/shard_map/all_gather | solution.py:552
  114.9 0.0 all-gather.3.cloned.1.call-done.weights_ref
  114.9 20.3 %shard_map.132.part_ref = f32[16,8,128]{2,1,0:T(8,128)} custom-call(s32[36864]{0:T(1024)} %bitcast.16, f32[128]{0:T(128)} %slice_bitcast_fusion.1.mean, bf16[16,1024,128]{2,1,0:T(8,128)(2,1)} %all-gather.3.cloned.1.call-done.weights_ref, f32[4096,128]{1,0:T(8,128)} %get-tuple-element.8.inc_ref, f32[256,2048]{1,0:T(8,128)} %bitcast.15, f32[8,2048]{1,0:T(8,128)} %area_ref.3), custom_call_target="tpu_custom_call" | custom-call | tf_op jit(solution)/shard_map/pallas_call | solution.py:575
  135.2 11.7 %shard_map.133 = (f32[16,8,128]{2,1,0:T(8,128)}, f32[8,128]{1,0:T(8,128)}) custom-call(f32[16,8,128]{2,1,0:T(8,128)} %shard_map.132.part_ref, f32[1,128]{1,0:T(1,128)} %bitcast.20, f32[1,128]{1,0:T(1,128)} %bitcast.21), custom_call_target="tpu_custom_call" | custom-call | tf_op jit(solution)/shard_map/pallas_call | solution.py:589
  146.9 1.4 slice.10
  148.4 10.6 %shard_map.134.grad_ref = f32[4096,128]{1,0:T(8,128)} custom-call(s32[36864]{0:T(1024)} %bitcast.17, f32[2048]{0:T(1024)} %bitcast.19, bf16[16,1024,128]{2,1,0:T(8,128)(2,1)} %all-gather.3.cloned.1.call-done.weights_ref), custom_call_target="tpu_custom_call" | custom-call | tf_op jit(solution)/shard_map/pallas_call | solution.py:598
  159.0 58.0 %shard_map.135 = f32[256,2048]{1,0:T(8,128)} custom-call(f32[4096,128]{1,0:T(8,128)} %shard_map.134.grad_ref, f32[128,128]{1,0:T(8,128)} %get-tuple-element.10.area_ref, f32[8,128]{1,0:T(8,128)} %get-tuple-element.7.totals_ref, f32[256,2048]{1,0:T(8,128)} %bitcast.13, f32[32,32]{1,0:T(8,128)} %time_ref.3, f32[128,128]{1,0:T(8,128)} %lat_ref.3, ...), custom_call_target="tpu_custom_call" | custom-call | tf_op jit(solution)/shard_map/pallas_call | solution.py:607
  217.0 1.2 slice_bitcast_fusion
  218.2 3.1 %copy.24 = f32[32,8,2048]{2,1,0:T(8,128)} copy(f32[32,8,2048]{2,1,0:T(8,128)} %bitcast.14) | data formatting | bytes 4194304
  (3 shorter events, 0.1 us)
Async XLA Ops:
  8.0 82.2 %sort.9.cloned.1.call-start = ((), (), s32[]{:S(2)}) async-start(), calls=%async_computation.1 | async-start | bytes 24608 | tf_op jit(solution)/shard_map/sort | solution.py:549
  10.8 104.1 %all-gather.3.cloned.1.call-start = ((), (), s32[]{:S(2)}) async-start(), calls=%async_computation | async-start | bytes 4456448 | tf_op jit(solution)/shard_map/all_gather | solution.py:541
Sparse Core Ops, SparseCore 0:
  11.8 5.5 sort.11.cloned.1.call-done
  (1 shorter events, 0.0 us)
Sparse Core Ops, SparseCore 1:
  13.6 67.3 all-gather.2
where the time goes:
time: 229 us
  Pallas kernels  178 us (78%)
  blocking collectives  23 us (10%)
  between operations  15.5 us (7%)
  local copies, waits for them, and re-layouts  8.33 us (4%)
  other arithmetic  3.04 us (1%)
    pallas_call x1, Pallas kernels, by_longitude(): pl.pallas_call(functools.partial(forward_kernel, devices), out_shape=(f32...  77.6 us
    pallas_call x1, Pallas kernels, by_longitude(): pl.pallas_call(functools.partial(adjoint_kernel, devices), out_shape=f32(...  58 us
    all_gather x1, blocking collectives, by_longitude(): lax.all_gather(jnp.concatenate([ordered, starts], axis=1).reshape(-1), 'c...  23 us
    pallas_call x1, Pallas kernels, by_longitude(): pl.pallas_call(functools.partial(share_kernel, devices, slots, foot), out...  20.3 us
    pallas_call x1, Pallas kernels, by_longitude(): pl.pallas_call(functools.partial(misfit_kernel, devices), out_shape=(f32(...  11.7 us
    pallas_call x1, Pallas kernels, by_longitude(): pl.pallas_call(functools.partial(scatter_kernel, devices, slots, foot), o...  10.6 us
  transfers between devices with their start and end apart: 1, of which 0 were waited for; matrix products, arithmetic and copies ran while one was open for 1% of the time, Pallas kernels for 34%

commit v1 on v0

--- a/solution.py
+++ b/solution.py
@@ -148,6 +148,39 @@
     return lax.broadcasted_iota(jnp.int32, shape, dim)
 
 
+def halves(value):
+    high = value.astype(jnp.bfloat16)
+    return high, (value - high.astype(jnp.float32)).astype(jnp.bfloat16)
+
+
+def product(left, right):
+    return lax.dot_general(left, right, (((1,), (0,)), ((), ())), preferred_element_type=jnp.float32)
+
+
+def stacked(value):
+    high, low = halves(value)
+    above = jnp.concatenate([high, low], axis=1)
+    below = jnp.concatenate([high, jnp.zeros_like(high)], axis=1)
+    return jnp.concatenate([above, below], axis=0)
+
+
+def fold(wide):
+    return wide[:, :LANES] + wide[:, LANES:]
+
+
+def left_wide(factor, data):
+    high, low = halves(data)
+    return fold(product(factor[0], jnp.concatenate([high, low], axis=1))) + product(factor[1], high)
+
+
+def left_square(factor, data):
+    return fold(product(jnp.concatenate(factor, axis=1), stacked(data)))
+
+
+def right_square(data, factor):
+    return fold(product(jnp.concatenate(halves(data), axis=1), factor))
+
+
 def spread_matrix(factor, repeat, adjoint):
     size = factor.shape[0]
     pick = (iota((size * repeat, size), 0) // repeat == iota((size * repeat, size), 1)).astype(jnp.float32)
@@ -194,34 +227,110 @@
     )
 
 
+class Travel:
+    def __init__(self, devices, me, own, everyone, send_sem, recv_sem):
+        self.devices, self.me, self.own, self.everyone = devices, me, own, everyone
+        self.send_sem, self.recv_sem = send_sem, recv_sem
+        self.steps = devices // 4
+        self.across = self.across_of(me)
+        self.core = me + 1 - 2 * lax.rem(me, 2)
+        self.copies = {}
+
+    def across_of(self, device):
+        return device + 2 - 4 * lax.rem(lax.div(device, 2), 2)
+
+    def behind(self, device, step):
+        return lax.rem(device - 4 * step + self.devices, self.devices)
+
+    def send(self, at, block, peer):
+        source = self.own if block is None else self.everyone.at[block]
+        copy = pltpu.make_async_remote_copy(
+            src_ref=source,
+            dst_ref=self.everyone.at[self.me if block is None else block],
+            send_sem=self.send_sem.at[at],
+            recv_sem=self.recv_sem.at[at],
+            device_id={"cells": peer},
+            device_id_type=pl.DeviceIdType.MESH,
+        )
+        copy.start()
+        self.copies[at] = copy
+
+    def start(self):
+        steps = self.steps
+        for step in range(1, steps):
+            self.send(step, None, lax.rem(self.me + 4 * step, self.devices))
+        self.send(steps, None, self.across)
+        self.send(2 * steps, None, self.core)
+        self.everyone[self.me] = self.own[...]
+
+    def arrived(self, at, block):
+        here = self.everyone.at[block]
+        pltpu.make_async_remote_copy(
+            src_ref=here,
+            dst_ref=here,
+            send_sem=self.send_sem.at[at],
+            recv_sem=self.recv_sem.at[at],
+            device_id={"cells": self.core},
+            device_id_type=pl.DeviceIdType.MESH,
+        ).wait_recv()
+
+    def first(self):
+        for step in range(1, self.steps):
+            block = self.behind(self.me, step)
+            self.arrived(step, block)
+            self.send(self.steps + step, block, self.across)
+            self.send(2 * self.steps + step, block, self.core)
+
+    def second(self):
+        for step in range(self.steps):
+            block = self.behind(self.across, step)
+            self.arrived(self.steps + step, block)
+            self.send(3 * self.steps + step, block, self.core)
+
+    def finish(self):
+        for step in range(self.steps):
+            self.arrived(2 * self.steps + step, self.behind(self.core, step))
+            self.arrived(3 * self.steps + step, self.behind(self.across_of(self.core), step))
+        for copy in self.copies.values():
+            copy.wait_send()
+
+
 def forward_kernel(
-    devices, x_ref, area_ref, time_ref, lat_ref, coarse_ref, fine_ref,
-    inc_ref, area_out, totals_ref,
-    work, sums, sendb, recvb, small_out, small_in, send_sem, recv_sem, small_send, small_recv,
+    devices, weights_ref, list_ref, x_ref, area_ref, time_ref, lat_ref, coarse_ref, fine_ref,
+    inc_ref, area_out, totals_ref, weights_out, list_out,
+    work, sums, sendb, recvb, small_out, small_in, list_in, send_sem, recv_sem, small_send, small_recv,
+    list_send, list_recv, travel_send, travel_recv,
 ):
     me = lax.axis_index("cells")
     rows = x_ref.shape[0]
     hours = time_ref.shape[0]
     chunk = rows // devices
-    time_wide = spread_matrix(time_ref[...], SUB, False)
-    coarse_wide = spread_matrix(coarse_ref[...], chunk, False)
+    greet(devices, me)
+    travel = Travel(devices, me, weights_ref, weights_out, travel_send, travel_recv)
+    travel.start()
+    copies = []
+    for step in range(1, devices):
+        copies.append(send_to(devices, me, step, list_ref, list_in.at[me], list_send.at[step], list_recv.at[step]))
+        copies[-1].start()
+    time_wide = halves(spread_matrix(time_ref[...], SUB, False))
+    coarse_wide = halves(spread_matrix(coarse_ref[...], chunk, False))
+    fine = stacked(fine_ref[...].T)
 
     def fine_step(p, carry):
         part = x_ref[:, pl.ds(pl.multiple_of(p * LANES, LANES), LANES)]
-        work[p] = dot(dot(time_wide, part, 1, 0), fine_ref[...], 1, 1)
-        return carry
-
-    lax.fori_loop(0, devices, fine_step, 0)
+        work[p] = right_square(left_wide(time_wide, part), fine)
+        return carry
+
+    lax.fori_loop(0, devices, fine_step, 0, unroll=2)
+    travel.first()
 
     def coarse_step(r, carry):
         at = pl.ds(pl.multiple_of(r * chunk, chunk), chunk)
-        mixed = dot(coarse_wide, work[:, at, :].reshape(devices * chunk, LANES), 1, 0).reshape(devices, chunk, LANES)
+        mixed = left_wide(coarse_wide, work[:, at, :].reshape(devices * chunk, LANES)).reshape(devices, chunk, LANES)
         sums[at, :] = jnp.sum(mixed, axis=0)
         return encode(mixed, carry, at, sendb, r)
 
-    scales = lax.fori_loop(0, devices, coarse_step, jnp.zeros((devices, SUB, LANES), jnp.float32))
-    greet(devices, me)
-    copies = []
+    scales = lax.fori_loop(0, devices, coarse_step, jnp.zeros((devices, SUB, LANES), jnp.float32), unroll=2)
     for step in range(1, devices):
         peer = lax.rem(me + step, devices)
         copies.append(send_to(devices, me, step, sendb.at[peer], recvb.at[me], send_sem.at[step], recv_sem.at[step]))
@@ -246,8 +355,11 @@
         copies[-1].start()
     recvb[me] = sendb[me]
     small_in[me] = small_out[me]
+    list_in[me] = list_ref[...]
+    travel.second()
     for copy in copies:
         copy.wait()
+    list_out[...] = list_in[...]
     total = small_in[0, SUB:SUB + 1]
     for p in range(1, devices):
         total = total + small_in[p, SUB:SUB + 1]
@@ -257,15 +369,16 @@
     for p in range(devices):
         area_out[SUB * p:SUB * (p + 1), :] = small_in[p, 0:SUB]
         work[p] = decode(recvb[p], small_in[p, 2 * SUB - 1:2 * SUB], chunk)
-    lat = lat_ref[...]
+    lat = halves(lat_ref[...])
 
     def lat_step(h, carry):
         at = pl.ds(pl.multiple_of(h * SUB, SUB), SUB)
         column = work[:, at, :].reshape(devices * SUB, LANES)
-        inc_ref[pl.ds(pl.multiple_of(h * LANES, LANES), LANES), :] = dot(lat, column, 1, 0)
+        inc_ref[pl.ds(pl.multiple_of(h * LANES, LANES), LANES), :] = left_square(lat, column)
         return carry
 
     lax.fori_loop(0, hours, lat_step, 0, unroll=4)
+    travel.finish()
 
 
 def share_kernel(
@@ -433,13 +546,13 @@
     rows = x_ref.shape[0]
     hours = time_ref.shape[0]
     chunk = rows // devices
-    lat = lat_ref[...].T
+    lat = halves(lat_ref[...].T)
     hour_sums[...] = jnp.zeros(hour_sums.shape, jnp.float32)
 
     def lat_step(h, carry):
         field = grad_ref[pl.ds(pl.multiple_of(h * LANES, LANES), LANES), :]
         at = pl.ds(pl.multiple_of(h * SUB, SUB), SUB)
-        work[:, at, :] = dot(lat, field, 1, 0).reshape(devices, SUB, LANES)
+        work[:, at, :] = left_square(lat, field).reshape(devices, SUB, LANES)
         hour_sums[pl.ds(h, 1), :] = jnp.sum(field * area_ref[...], axis=0, keepdims=True)
         return carry
 
@@ -449,7 +562,7 @@
         at = pl.ds(pl.multiple_of(r * chunk, chunk), chunk)
         return encode(work[:, at, :], carry, at, sendb, r)
 
-    scales = lax.fori_loop(0, devices, encode_step, jnp.zeros((devices, SUB, LANES), jnp.float32))
+    scales = lax.fori_loop(0, devices, encode_step, jnp.zeros((devices, SUB, LANES), jnp.float32), unroll=2)
     greet(devices, me)
     copies = []
     for step in range(1, devices):
@@ -468,8 +581,9 @@
         copies[-1].start()
     small_in[me] = small_out[me]
     recvb[me] = sendb[me]
-    time_wide = spread_matrix(time_ref[...], SUB, True)
-    coarse_wide = spread_matrix(coarse_ref[...], chunk, True)
+    time_wide = halves(spread_matrix(time_ref[...], SUB, True))
+    coarse_wide = halves(spread_matrix(coarse_ref[...], chunk, True))
+    fine = stacked(fine_ref[...])
     square = jnp.ones((LANES, LANES), jnp.float32)
     lat_sums = dot(square, lat_ref[...], 1, 0)
     place = (iota((rows, LANES), 1) == SUB * me + iota((rows, LANES), 0) % SUB).astype(jnp.float32)
@@ -488,19 +602,19 @@
 
     def coarse_step(r, carry):
         at = pl.ds(pl.multiple_of(r * chunk, chunk), chunk)
-        mixed[:, at, :] = dot(coarse_wide, work[:, at, :].reshape(devices * chunk, LANES), 1, 0).reshape(
+        mixed[:, at, :] = left_wide(coarse_wide, work[:, at, :].reshape(devices * chunk, LANES)).reshape(
             devices, chunk, LANES
         )
         return carry
 
-    lax.fori_loop(0, devices, coarse_step, 0)
+    lax.fori_loop(0, devices, coarse_step, 0, unroll=2)
 
     def fine_step(p, carry):
         lanes = pl.ds(pl.multiple_of(p * LANES, LANES), LANES)
-        out_ref[:, lanes] = x_ref[:, lanes] + dot(time_wide, dot(mixed[p], fine_ref[...], 1, 0), 1, 0)
-        return carry
-
-    lax.fori_loop(0, devices, fine_step, 0)
+        out_ref[:, lanes] = x_ref[:, lanes] + left_wide(time_wide, right_square(mixed[p], fine))
+        return carry
+
+    lax.fori_loop(0, devices, fine_step, 0, unroll=2)
 
 
 def f32(*shape):
@@ -538,7 +652,6 @@
     soundings = footprint_tiles.shape[0]
     cells = hours * latitude
 
-    gathered = lax.all_gather(footprint_weights.reshape(slots, LANES), "cells", axis=0, tiled=False)
     tiles = footprint_tiles.reshape(-1)
     hour = footprint_hours.reshape(-1)
     lat = tiles // devices
@@ -549,18 +662,26 @@
     ordered = lax.sort(jnp.stack([by_lon, by_lat]), dimension=1)
     edges = jnp.arange(LANES, dtype=jnp.int32) * (cells * slots)
     starts = jnp.sum((ordered[:, None, :] < edges[None, :, None]).astype(jnp.int32), axis=2)
-    lists = lax.all_gather(jnp.concatenate([ordered, starts], axis=1).reshape(-1), "cells", axis=0, tiled=True)
+    room = jnp.zeros((2, 3 * LANES), jnp.int32)
+    listed = jnp.concatenate([ordered, starts, room], axis=1).reshape(-1, LANES)
 
     x = control.reshape(rows, longitude)
     prior = prior_flux.reshape(rows, longitude)
     sems = [pltpu.SemaphoreType.DMA((devices,))] * 4
     blocks = (devices, rows, LANES)
     limits = dict(vmem_limit_bytes=MESH_BUDGET, has_side_effects=True)
-    increment, area_column, totals = pl.pallas_call(
+    every_list = (devices,) + listed.shape
+    increment, area_column, totals, gathered, lists = pl.pallas_call(
         functools.partial(forward_kernel, devices),
-        out_shape=(f32(cells, LANES), f32(latitude, LANES), f32(SUB, LANES)),
-        in_specs=vmem(6),
-        out_specs=tuple(vmem(3)),
+        out_shape=(
+            f32(cells, LANES),
+            f32(latitude, LANES),
+            f32(SUB, LANES),
+            jax.ShapeDtypeStruct((devices, slots, LANES), jnp.bfloat16),
+            jax.ShapeDtypeStruct(every_list, jnp.int32),
+        ),
+        in_specs=vmem(8),
+        out_specs=tuple(vmem(5)),
         scratch_shapes=[
             pltpu.VMEM(blocks, jnp.float32),
             pltpu.VMEM((rows, LANES), jnp.float32),
@@ -568,10 +689,12 @@
             pltpu.VMEM(blocks, jnp.int16),
             pltpu.VMEM((devices, 2 * SUB, LANES), jnp.float32),
             pltpu.VMEM((devices, 2 * SUB, LANES), jnp.float32),
-        ] + sems,
+            pltpu.VMEM(every_list, jnp.int32),
+        ] + sems + sems,
         compiler_params=pltpu.CompilerParams(collective_id=0, **limits),
-    )(x, area_weight, time_factor, lat_factor, coarse_lon, fine_lon)
-
+    )(footprint_weights.reshape(slots, LANES), listed, x, area_weight, time_factor, lat_factor, coarse_lon, fine_lon)
+
+    lists = lists.reshape(-1)
     partial = pl.pallas_call(
         functools.partial(share_kernel, devices, slots, foot),
         out_shape=f32(devices, SUB, soundings),
@@ -626,6 +749,7 @@
 def fits(devices, control, coarse_lon, fine_lon, lat_factor, footprint_tiles):
     return (
         devices == coarse_lon.shape[0]
+        and devices % 4 == 0
         and fine_lon.shape[0] == LANES
         and control.shape[1] == SUB
         and lat_factor.shape[0] == LANES

time: 229 us -> 198 us (0.86)
  blocking collectives: 23 us -> 0 us
  Pallas kernels: 178 us -> 163 us
  local copies, waits for them, and re-layouts: 8.33 us -> 15.8 us
    all_gather x1 -> x0, blocking collectives: 23 us -> none  [by_longitude(): lax.all_gather(jnp.concatenate([ordered, starts], axis=1).reshape(-1), 'c...]
    pallas_call x1, Pallas kernels: 58 us -> 46.4 us  [by_longitude(): pl.pallas_call(functools.partial(adjoint_kernel, devices), out_shape=f32(...]
    pallas_call x1, Pallas kernels: 77.6 us -> 68 us  [by_longitude(): pl.pallas_call(functools.partial(forward_kernel, devices), out_shape=(f32...]
    sort x2, local copies, waits for them, and re-layouts: 0.04 us -> 6.94 us  [by_longitude(): ordered = lax.sort(jnp.stack([by_lon, by_lat]), dimension=1)]
    pallas_call x1, Pallas kernels: 11.7 us -> 18 us  [by_longitude(): pl.pallas_call(functools.partial(misfit_kernel, devices), out_shape=(f32(...]
  transfers between devices with their start and end apart: 1 -> 0, of which waited for: 0 -> 0; matrix products, arithmetic and copies ran while one was open for 1% -> 0% of each run, Pallas kernels for 34% -> 0%
where the time goes in v1:
time: 198 us; the launch traced here: 196 us
  Pallas kernels  163 us (82%)
  local copies, waits for them, and re-layouts  15.8 us (8%)
  between operations  14.1 us (7%)
  other arithmetic  3.05 us (2%)
    pallas_call x1, Pallas kernels, by_longitude(): pl.pallas_call(functools.partial(forward_kernel, devices), out_shape=(f32...  68 us
    pallas_call x1, Pallas kernels, by_longitude(): pl.pallas_call(functools.partial(adjoint_kernel, devices), out_shape=f32(...  46.4 us
    pallas_call x1, Pallas kernels, by_longitude(): pl.pallas_call(functools.partial(share_kernel, devices, slots, foot), out...  19.5 us
    pallas_call x1, Pallas kernels, by_longitude(): pl.pallas_call(functools.partial(misfit_kernel, devices), out_shape=(f32(...  18 us
    pallas_call x1, Pallas kernels, by_longitude(): pl.pallas_call(functools.partial(scatter_kernel, devices, slots, foot), o...  11.4 us
    sort x2, local copies, waits for them, and re-layouts, by_longitude(): ordered = lax.sort(jnp.stack([by_lon, by_lat]), dimension=1)  6.94 us

profile of v1, /device:TPU:0, one launch (start us, length us, event | category | flops | bytes accessed | tf_op | source)
XLA Modules:
  0.0 196.2 jit_solution(13698937072951535399)
XLA Ops:
  7.2 0.0 sort.9.cloned.1.call-start
  7.2 0.7 broadcast_multiply_fusion.1
  7.9 0.1 copy.18
  8.0 0.1 mul.96
  8.1 0.1 copy.19
  8.2 0.1 mul.102
  8.3 0.8 copy.17
  9.1 0.1 reshape.281
  9.2 0.1 iota_add_fusion
  9.3 0.6 pad_add_fusion
  9.9 0.0 sort.9.cloned.1.call-update
  10.0 6.9 %sort.9.cloned.1.call-done = s32[2,1024]{1,0:T(2,128)} async-done(((s32[2,1024]{1,0:T(2,128)}), s32[2,1024]{1,0:T(2,128)}) %sort.9.cloned.1.call-update) | async-done | bytes 8208 | tf_op jit(solution)/shard_map/sort | solution.py:662
  16.9 0.9 convert_reduce_fusion
  17.8 0.7 add_add_fusion
  18.5 0.6 reshape.282.list_ref
  19.1 68.0 %shard_map.131 = (f32[4096,128]{1,0:T(8,128)}, f32[128,128]{1,0:T(8,128)}, f32[8,128]{1,0:T(8,128)}, bf16[16,1024,128]{2,1,0:T(8,128)(2,1)}, s32[16,24,128]{2,1,0:T(8,128)}) custom-call(bf16[1024,128]{1,0:T(8,128)(2,1)} %bitcast.18, s32[24,128]{1,0:T(8,128)} %reshape.282.list_ref, f32[256,2048]{1,0:T(8,128)} %bitcast.12, f32[8,2048]{1,0:T(8,128)} %area_ref.3, ...), custom_call_target="tpu_custom_call" | custom-call | tf_op jit(solution)/shard_map/pallas_call | solution.py:674
  87.1 1.2 slice_bitcast_fusion.1.mean
  88.3 19.5 %shard_map.132.part_ref = f32[16,8,128]{2,1,0:T(8,128)} custom-call(s32[49152]{0:T(1024)} %bitcast.16, f32[128]{0:T(128)} %slice_bitcast_fusion.1.mean, bf16[16,1024,128]{2,1,0:T(8,128)(2,1)} %get-tuple-element.11.weights_ref, f32[4096,128]{1,0:T(8,128)} %get-tuple-element.12.inc_ref, f32[256,2048]{1,0:T(8,128)} %bitcast.15, f32[8,2048]{1,0:T(8,128)} %area_ref.3), custom_call_target="tpu_custom_call" | custom-call | tf_op jit(solution)/shard_map/pallas_call | solution.py:698
  107.8 18.0 %shard_map.133 = (f32[16,8,128]{2,1,0:T(8,128)}, f32[8,128]{1,0:T(8,128)}) custom-call(f32[16,8,128]{2,1,0:T(8,128)} %shard_map.132.part_ref, f32[1,128]{1,0:T(1,128)} %bitcast.20, f32[1,128]{1,0:T(1,128)} %bitcast.21), custom_call_target="tpu_custom_call" | custom-call | tf_op jit(solution)/shard_map/pallas_call | solution.py:712
  125.8 1.4 slice.10
  127.3 11.4 %shard_map.134.grad_ref = f32[4096,128]{1,0:T(8,128)} custom-call(s32[49152]{0:T(1024)} %bitcast.17, f32[2048]{0:T(1024)} %bitcast.19, bf16[16,1024,128]{2,1,0:T(8,128)(2,1)} %get-tuple-element.11.weights_ref), custom_call_target="tpu_custom_call" | custom-call | tf_op jit(solution)/shard_map/pallas_call | solution.py:721
  138.7 46.4 %shard_map.135 = f32[256,2048]{1,0:T(8,128)} custom-call(f32[4096,128]{1,0:T(8,128)} %shard_map.134.grad_ref, f32[128,128]{1,0:T(8,128)} %get-tuple-element.14.area_ref, f32[8,128]{1,0:T(8,128)} %get-tuple-element.10.totals_ref, f32[256,2048]{1,0:T(8,128)} %bitcast.13, f32[32,32]{1,0:T(8,128)} %time_ref.3, f32[128,128]{1,0:T(8,128)} %lat_ref.3, ...), custom_call_target="tpu_custom_call" | custom-call | tf_op jit(solution)/shard_map/pallas_call | solution.py:730
  185.0 1.2 slice_bitcast_fusion
  186.2 3.1 %copy.21 = f32[32,8,2048]{2,1,0:T(8,128)} copy(f32[32,8,2048]{2,1,0:T(8,128)} %bitcast.14) | data formatting | bytes 4194304
  (4 shorter events, 0.1 us)
Async XLA Ops:
  7.2 9.7 %sort.9.cloned.1.call-start = ((), (), s32[]{:S(2)}) async-start(), calls=%async_computation | async-start | bytes 24608 | tf_op jit(solution)/shard_map/sort | solution.py:662
Sparse Core Ops, SparseCore 0:
  11.0 5.5 sort.11.cloned.1.call-done
  (1 shorter events, 0.0 us)

commit v2 on v1

--- a/solution.py
+++ b/solution.py
@@ -195,9 +195,9 @@
     return jnp.where(iota(scales.shape, 2) == column, largest * (1.0 / 32767.0), scales)
 
 
-def decode(coded, steps, chunk):
+def decode(coded, steps, chunk, first):
     rows = coded.shape[0]
-    pick = (iota((rows, LANES), 1) == iota((rows, LANES), 0) // chunk).astype(jnp.float32)
+    pick = (iota((rows, LANES), 1) == (iota((rows, LANES), 0) + first) // chunk).astype(jnp.float32)
     return coded.astype(jnp.int32).astype(jnp.float32) * dot(pick, jnp.broadcast_to(steps, (LANES, LANES)), 1, 1)
 
 
@@ -214,6 +214,20 @@
             barrier, inc=1, device_id={"cells": lax.rem(me + step, devices)}, device_id_type=pl.DeviceIdType.MESH
         )
     pl.semaphore_wait(barrier, devices - 1)
+
+
+def send_half(devices, me, half, sendb, recvb, send_sem, recv_sem):
+    rows = sendb.shape[1] // 2
+    part = pl.ds(half * rows, rows)
+    copies = []
+    for step in range(1, devices):
+        peer = lax.rem(me + step, devices)
+        source, target = sendb.at[peer, part], recvb.at[me, part]
+        copies.append(
+            send_to(devices, me, step, source, target, send_sem.at[half, step], recv_sem.at[half, step])
+        )
+        copies[-1].start()
+    return copies
 
 
 def send_to(devices, me, step, source, target, send_sem, recv_sem):
@@ -232,9 +246,9 @@
         self.devices, self.me, self.own, self.everyone = devices, me, own, everyone
         self.send_sem, self.recv_sem = send_sem, recv_sem
         self.steps = devices // 4
+        self.z = lax.div(me, 4)
         self.across = self.across_of(me)
         self.core = me + 1 - 2 * lax.rem(me, 2)
-        self.copies = {}
 
     def across_of(self, device):
         return device + 2 - 4 * lax.rem(lax.div(device, 2), 2)
@@ -242,62 +256,70 @@
     def behind(self, device, step):
         return lax.rem(device - 4 * step + self.devices, self.devices)
 
-    def send(self, at, block, peer):
-        source = self.own if block is None else self.everyone.at[block]
-        copy = pltpu.make_async_remote_copy(
-            src_ref=source,
-            dst_ref=self.everyone.at[self.me if block is None else block],
-            send_sem=self.send_sem.at[at],
+    def inside(self, z):
+        return (z >= 0) & (z < self.steps)
+
+    def copy(self, at, block, peer, lane=0):
+        return pltpu.make_async_remote_copy(
+            src_ref=self.everyone.at[block],
+            dst_ref=self.everyone.at[block],
+            send_sem=self.send_sem.at[at + lane],
             recv_sem=self.recv_sem.at[at],
             device_id={"cells": peer},
             device_id_type=pl.DeviceIdType.MESH,
         )
-        copy.start()
-        self.copies[at] = copy
+
+    def onward(self, direction, hops):
+        block = self.me - 4 * direction * hops
+        at, lane = (hops + 1, 0) if direction > 0 else (self.steps - 1 - hops, self.devices)
+        return self.copy(at, block, self.me + 4 * direction, lane), self.inside(self.z + direction)
 
     def start(self):
-        steps = self.steps
-        for step in range(1, steps):
-            self.send(step, None, lax.rem(self.me + 4 * step, self.devices))
-        self.send(steps, None, self.across)
-        self.send(2 * steps, None, self.core)
         self.everyone[self.me] = self.own[...]
-
-    def arrived(self, at, block):
-        here = self.everyone.at[block]
-        pltpu.make_async_remote_copy(
-            src_ref=here,
-            dst_ref=here,
-            send_sem=self.send_sem.at[at],
-            recv_sem=self.recv_sem.at[at],
-            device_id={"cells": self.core},
-            device_id_type=pl.DeviceIdType.MESH,
-        ).wait_recv()
-
-    def first(self):
-        for step in range(1, self.steps):
-            block = self.behind(self.me, step)
-            self.arrived(step, block)
-            self.send(self.steps + step, block, self.across)
-            self.send(2 * self.steps + step, block, self.core)
+        for direction in (1, -1):
+            copy, there = self.onward(direction, 0)
+            pl.when(there)(copy.start)
+        self.copy(self.steps, self.me, self.across).start()
+        self.copy(2 * self.steps, self.me, self.core).start()
+
+    def arrive(self, hops):
+        for direction in (1, -1):
+            block = self.me - 4 * direction * hops
+            at = hops if direction > 0 else self.steps - hops
+
+            @pl.when(self.inside(self.z - direction * hops))
+            def _():
+                self.copy(at, block, self.core).wait_recv()
+                if hops < self.steps - 1:
+                    copy, there = self.onward(direction, hops)
+                    pl.when(there)(copy.start)
+                self.copy(self.steps + at, block, self.across).start()
+                self.copy(2 * self.steps + at, block, self.core).start()
 
     def second(self):
         for step in range(self.steps):
             block = self.behind(self.across, step)
-            self.arrived(self.steps + step, block)
-            self.send(3 * self.steps + step, block, self.core)
+            self.copy(self.steps + step, block, self.core).wait_recv()
+            self.copy(3 * self.steps + step, block, self.core).start()
 
     def finish(self):
         for step in range(self.steps):
-            self.arrived(2 * self.steps + step, self.behind(self.core, step))
-            self.arrived(3 * self.steps + step, self.behind(self.across_of(self.core), step))
-        for copy in self.copies.values():
-            copy.wait_send()
+            self.copy(2 * self.steps + step, self.behind(self.core, step), self.core).wait_recv()
+            self.copy(3 * self.steps + step, self.behind(self.across_of(self.core), step), self.core).wait_recv()
+        for step in range(self.steps):
+            block = self.behind(self.me, step)
+            self.copy(self.steps + step, block, self.across).wait_send()
+            self.copy(2 * self.steps + step, block, self.core).wait_send()
+            self.copy(3 * self.steps + step, self.behind(self.across, step), self.core).wait_send()
+        for direction in (1, -1):
+            for hops in range(self.steps - 1):
+                copy, there = self.onward(direction, hops)
+                pl.when(there & self.inside(self.z - direction * hops))(copy.wait_send)
 
 
 def forward_kernel(
-    devices, weights_ref, list_ref, x_ref, area_ref, time_ref, lat_ref, coarse_ref, fine_ref,
-    inc_ref, area_out, totals_ref, weights_out, list_out,
+    devices, weights_ref, list_ref, seen_ref, variance_ref, x_ref, area_ref, time_ref, lat_ref, coarse_ref, fine_ref,
+    inc_ref, area_out, totals_ref, weights_out, list_out, seen_out, variance_out,
     work, sums, sendb, recvb, small_out, small_in, list_in, send_sem, recv_sem, small_send, small_recv,
     list_send, list_recv, travel_send, travel_recv,
 ):
@@ -322,7 +344,7 @@
         return carry
 
     lax.fori_loop(0, devices, fine_step, 0, unroll=2)
-    travel.first()
+    travel.arrive(1)
 
     def coarse_step(r, carry):
         at = pl.ds(pl.multiple_of(r * chunk, chunk), chunk)
@@ -330,12 +352,12 @@
         sums[at, :] = jnp.sum(mixed, axis=0)
         return encode(mixed, carry, at, sendb, r)
 
-    scales = lax.fori_loop(0, devices, coarse_step, jnp.zeros((devices, SUB, LANES), jnp.float32), unroll=2)
-    for step in range(1, devices):
-        peer = lax.rem(me + step, devices)
-        copies.append(send_to(devices, me, step, sendb.at[peer], recvb.at[me], send_sem.at[step], recv_sem.at[step]))
-        copies[-1].start()
-
+    scales = jnp.zeros((devices, SUB, LANES), jnp.float32)
+    sent = []
+    for half in range(2):
+        middle = devices // 2
+        scales = lax.fori_loop(half * middle, (half + 1) * middle, coarse_step, scales, unroll=2)
+        sent.append(send_half(devices, me, half, sendb, recvb, send_sem, recv_sem))
     ones = jnp.ones((SUB, LANES), jnp.float32)
     lat_sums = dot(ones, lat_ref[...], 1, 0)
     place = (iota((LANES, rows), 0) == SUB * me + iota((LANES, rows), 1) % SUB).astype(jnp.float32)
@@ -347,6 +369,8 @@
     for p in range(devices):
         small_out[p, 0:SUB] = area_ref[:, p * LANES:(p + 1) * LANES]
         small_out[p, SUB:2 * SUB] = jnp.where(iota((SUB, LANES), 0) < SUB // 2, mine, scales[p])
+        small_out[p, SUB + 1:SUB + 2] = seen_ref[...]
+        small_out[p, SUB + 2:SUB + 3] = variance_ref[...]
     for step in range(1, devices):
         peer = lax.rem(me + step, devices)
         copies.append(
@@ -356,6 +380,8 @@
     recvb[me] = sendb[me]
     small_in[me] = small_out[me]
     list_in[me] = list_ref[...]
+    for hops in range(2, travel.steps):
+        travel.arrive(hops)
     travel.second()
     for copy in copies:
         copy.wait()
@@ -368,7 +394,8 @@
     totals_ref[...] = jnp.where(iota((SUB, LANES), 1) == hours, total, total / weight)
     for p in range(devices):
         area_out[SUB * p:SUB * (p + 1), :] = small_in[p, 0:SUB]
-        work[p] = decode(recvb[p], small_in[p, 2 * SUB - 1:2 * SUB], chunk)
+        seen_out[p:p + 1, :] = small_in[p, SUB + 1:SUB + 2]
+        variance_out[p:p + 1, :] = small_in[p, SUB + 2:SUB + 3]
     lat = halves(lat_ref[...])
 
     def lat_step(h, carry):
@@ -377,7 +404,14 @@
         inc_ref[pl.ds(pl.multiple_of(h * LANES, LANES), LANES), :] = left_square(lat, column)
         return carry
 
-    lax.fori_loop(0, hours, lat_step, 0, unroll=4)
+    for half in range(2):
+        for copy in sent[half]:
+            copy.wait()
+        first = half * (rows // 2)
+        part = slice(first, first + rows // 2)
+        for p in range(devices):
+            work[p, part] = decode(recvb[p, part], small_in[p, 2 * SUB - 1:2 * SUB], chunk, first)
+        lax.fori_loop(half * (hours // 2), (half + 1) * (hours // 2), lat_step, 0, unroll=4)
     travel.finish()
 
 
@@ -455,40 +489,26 @@
         for k in range(1, foot):
             at = pl.multiple_of(k * devices * soundings + s * soundings, soundings)
             summed = summed + shares[pl.ds(at, soundings), :]
-        out_ref[s] = dot(ones, summed, 1, 1)
+        out_ref[pl.ds(s, 1), :] = dot(ones, summed, 1, 1)[0:1]
         return carry
 
     lax.fori_loop(0, devices, collect, 0)
 
 
-def misfit_kernel(
-    devices, part_ref, seen_ref, variance_ref, all_ref, own_ref,
-    got, spread, mine, send_sem, recv_sem, back_send, back_recv,
-):
+def misfit_kernel(devices, part_ref, seen_ref, variance_ref, all_ref, got, send_sem, recv_sem):
     me = lax.axis_index("cells")
     greet(devices, me)
     copies = []
     for step in range(1, devices):
-        peer = lax.rem(me + step, devices)
-        copies.append(send_to(devices, me, step, part_ref.at[peer], got.at[me], send_sem.at[step], recv_sem.at[step]))
+        copies.append(send_to(devices, me, step, part_ref, got.at[me], send_sem.at[step], recv_sem.at[step]))
         copies[-1].start()
-    got[me] = part_ref[me]
+    got[me] = part_ref[...]
     for copy in copies:
         copy.wait()
     predicted = got[0]
     for p in range(1, devices):
         predicted = predicted + got[p]
-    misfit = (predicted - seen_ref[...]) / variance_ref[...]
-    mine[...] = misfit
-    copies = []
-    for step in range(1, devices):
-        copies.append(send_to(devices, me, step, mine, spread.at[me], back_send.at[step], back_recv.at[step]))
-        copies[-1].start()
-    spread[me] = misfit
-    own_ref[...] = misfit
-    for copy in copies:
-        copy.wait()
-    all_ref[...] = spread[...]
+    all_ref[...] = (predicted - seen_ref[...]) / variance_ref[...]
 
 
 def scatter_kernel(devices, slots, foot, lists, misfit, weights_ref, grad_ref, wide):
@@ -539,11 +559,11 @@
 
 
 def adjoint_kernel(
-    devices, grad_ref, area_ref, totals_ref, x_ref, time_ref, lat_ref, coarse_ref, fine_ref, out_ref,
+    devices, grad_ref, area_ref, totals_ref, time_ref, lat_ref, coarse_ref, fine_ref, out_ref,
     work, mixed, hour_sums, sendb, recvb, small_out, small_in, send_sem, recv_sem, small_send, small_recv,
 ):
     me = lax.axis_index("cells")
-    rows = x_ref.shape[0]
+    rows = out_ref.shape[0]
     hours = time_ref.shape[0]
     chunk = rows // devices
     lat = halves(lat_ref[...].T)
@@ -556,19 +576,19 @@
         hour_sums[pl.ds(h, 1), :] = jnp.sum(field * area_ref[...], axis=0, keepdims=True)
         return carry
 
-    lax.fori_loop(0, hours, lat_step, 0, unroll=4)
-
     def encode_step(r, carry):
         at = pl.ds(pl.multiple_of(r * chunk, chunk), chunk)
         return encode(work[:, at, :], carry, at, sendb, r)
 
-    scales = lax.fori_loop(0, devices, encode_step, jnp.zeros((devices, SUB, LANES), jnp.float32), unroll=2)
     greet(devices, me)
+    scales = jnp.zeros((devices, SUB, LANES), jnp.float32)
+    sent = []
+    for half in range(2):
+        middle = devices // 2
+        lax.fori_loop(half * (hours // 2), (half + 1) * (hours // 2), lat_step, 0, unroll=4)
+        scales = lax.fori_loop(half * middle, (half + 1) * middle, encode_step, scales, unroll=2)
+        sent.append(send_half(devices, me, half, sendb, recvb, send_sem, recv_sem))
     copies = []
-    for step in range(1, devices):
-        peer = lax.rem(me + step, devices)
-        copies.append(send_to(devices, me, step, sendb.at[peer], recvb.at[me], send_sem.at[step], recv_sem.at[step]))
-        copies[-1].start()
     ones = jnp.ones((SUB, LANES), jnp.float32)
     weighted = dot(ones, hour_sums[...], 1, 1)
     for p in range(devices):
@@ -597,9 +617,6 @@
     hour_of = (iota((rows, LANES), 1) == iota((rows, LANES), 0) // SUB).astype(jnp.float32)
     level_column = dot(hour_of, jnp.broadcast_to(level, (LANES, LANES)), 1, 1)
     shift = lat_column * level_column
-    for p in range(devices):
-        work[p] = decode(recvb[p], small_in[p, SUB - 1:SUB], chunk) - shift
-
     def coarse_step(r, carry):
         at = pl.ds(pl.multiple_of(r * chunk, chunk), chunk)
         mixed[:, at, :] = left_wide(coarse_wide, work[:, at, :].reshape(devices * chunk, LANES)).reshape(
@@ -607,11 +624,18 @@
         )
         return carry
 
-    lax.fori_loop(0, devices, coarse_step, 0, unroll=2)
+    for half in range(2):
+        for copy in sent[half]:
+            copy.wait()
+        first = half * (rows // 2)
+        part = slice(first, first + rows // 2)
+        for p in range(devices):
+            work[p, part] = decode(recvb[p, part], small_in[p, SUB - 1:SUB], chunk, first) - shift[part]
+        lax.fori_loop(half * (devices // 2), (half + 1) * (devices // 2), coarse_step, 0, unroll=2)
 
     def fine_step(p, carry):
         lanes = pl.ds(pl.multiple_of(p * LANES, LANES), LANES)
-        out_ref[:, lanes] = x_ref[:, lanes] + left_wide(time_wide, right_square(mixed[p], fine))
+        out_ref[:, lanes] = left_wide(time_wide, right_square(mixed[p], fine))
         return carry
 
     lax.fori_loop(0, devices, fine_step, 0, unroll=2)
@@ -667,11 +691,14 @@
 
     x = control.reshape(rows, longitude)
     prior = prior_flux.reshape(rows, longitude)
-    sems = [pltpu.SemaphoreType.DMA((devices,))] * 4
+    pair = [pltpu.SemaphoreType.DMA((devices,))] * 2
+    sems = [pltpu.SemaphoreType.DMA((2, devices))] * 2 + pair
+    seen = observations.reshape(1, soundings)
+    variance = error_variance.reshape(1, soundings)
     blocks = (devices, rows, LANES)
     limits = dict(vmem_limit_bytes=MESH_BUDGET, has_side_effects=True)
     every_list = (devices,) + listed.shape
-    increment, area_column, totals, gathered, lists = pl.pallas_call(
+    increment, area_column, totals, gathered, lists, every_seen, every_variance = pl.pallas_call(
         functools.partial(forward_kernel, devices),
         out_shape=(
             f32(cells, LANES),
@@ -679,9 +706,11 @@
             f32(SUB, LANES),
             jax.ShapeDtypeStruct((devices, slots, LANES), jnp.bfloat16),
             jax.ShapeDtypeStruct(every_list, jnp.int32),
+            f32(devices, soundings),
+            f32(devices, soundings),
         ),
-        in_specs=vmem(8),
-        out_specs=tuple(vmem(5)),
+        in_specs=vmem(10),
+        out_specs=tuple(vmem(7)),
         scratch_shapes=[
             pltpu.VMEM(blocks, jnp.float32),
             pltpu.VMEM((rows, LANES), jnp.float32),
@@ -690,14 +719,14 @@
             pltpu.VMEM((devices, 2 * SUB, LANES), jnp.float32),
             pltpu.VMEM((devices, 2 * SUB, LANES), jnp.float32),
             pltpu.VMEM(every_list, jnp.int32),
-        ] + sems + sems,
+        ] + sems + pair + [pltpu.SemaphoreType.DMA((2 * devices,))] * 2,
         compiler_params=pltpu.CompilerParams(collective_id=0, **limits),
-    )(footprint_weights.reshape(slots, LANES), listed, x, area_weight, time_factor, lat_factor, coarse_lon, fine_lon)
+    )(footprint_weights.reshape(slots, LANES), listed, seen, variance, x, area_weight, time_factor, lat_factor, coarse_lon, fine_lon)
 
     lists = lists.reshape(-1)
     partial = pl.pallas_call(
         functools.partial(share_kernel, devices, slots, foot),
-        out_shape=f32(devices, SUB, soundings),
+        out_shape=f32(devices, soundings),
         in_specs=smem(2) + vmem(4),
         out_specs=vmem(1)[0],
         scratch_shapes=[
@@ -709,14 +738,14 @@
     )(lists, totals[0], gathered, increment, prior, area_weight)
 
     small = pltpu.VMEM((devices, SUB, LANES), jnp.float32)
-    every, own = pl.pallas_call(
+    every = pl.pallas_call(
         functools.partial(misfit_kernel, devices),
-        out_shape=(f32(devices, SUB, soundings), f32(SUB, soundings)),
+        out_shape=f32(devices, soundings),
         in_specs=vmem(3),
-        out_specs=tuple(vmem(2)),
-        scratch_shapes=[small, small, pltpu.VMEM((SUB, LANES), jnp.float32)] + sems,
+        out_specs=vmem(1)[0],
+        scratch_shapes=[pltpu.VMEM((devices, devices, soundings), jnp.float32)] + pair,
         compiler_params=pltpu.CompilerParams(collective_id=1, **limits),
-    )(partial, observations.reshape(1, soundings), error_variance.reshape(1, soundings))
+    )(partial, every_seen, every_variance)
 
     grad = pl.pallas_call(
         functools.partial(scatter_kernel, devices, slots, foot),
@@ -725,12 +754,12 @@
         out_specs=vmem(1)[0],
         scratch_shapes=[pltpu.VMEM((devices * slots, LANES), jnp.float32)],
         compiler_params=pltpu.CompilerParams(vmem_limit_bytes=MESH_BUDGET),
-    )(lists, every[:, 0].reshape(-1), gathered)
-
-    gradient = pl.pallas_call(
+    )(lists, every.reshape(-1), gathered)
+
+    back = pl.pallas_call(
         functools.partial(adjoint_kernel, devices),
         out_shape=f32(rows, longitude),
-        in_specs=vmem(8),
+        in_specs=vmem(7),
         out_specs=vmem(1)[0],
         scratch_shapes=[
             pltpu.VMEM(blocks, jnp.float32),
@@ -742,8 +771,9 @@
             small,
         ] + sems,
         compiler_params=pltpu.CompilerParams(collective_id=2, **limits),
-    )(grad, area_column, totals, x, time_factor, lat_factor, coarse_lon, fine_lon)
-    return gradient.reshape(control.shape), own[0]
+    )(grad, area_column, totals, time_factor, lat_factor, coarse_lon, fine_lon)
+    own = lax.dynamic_index_in_dim(every, lax.axis_index("cells"), keepdims=False)
+    return control + back.reshape(control.shape), own
 
 
 def fits(devices, control, coarse_lon, fine_lon, lat_factor, footprint_tiles):

time: 198 us -> 188 us (0.949); the launches traced: 196 us -> 188 us
  Pallas kernels: 163 us -> 157 us
  local copies, waits for them, and re-layouts: 15.8 us -> 11.2 us
  other arithmetic: 3.05 us -> 6.3 us
    pallas_call x1, Pallas kernels: 18 us -> 8.14 us  [by_longitude(): pl.pallas_call(functools.partial(misfit_kernel, devices), out_shape=f32(d...]
    add x0 -> x1, other arithmetic: none -> 3.25 us  [by_longitude(): return (control + back.reshape(control.shape), own)]
    unnamed x3 -> x4, local copies, waits for them, and re-layouts: 3.94 us -> 0.81 us
    pallas_call x1, Pallas kernels: 19.5 us -> 22.5 us  [by_longitude(): pl.pallas_call(functools.partial(share_kernel, devices, slots, foot), out...]
where the time goes in v2:
time: 188 us
  Pallas kernels  157 us (84%)
  between operations  14.1 us (8%)
  local copies, waits for them, and re-layouts  11.2 us (6%)
  other arithmetic  6.3 us (3%)
    pallas_call x1, Pallas kernels, by_longitude(): pl.pallas_call(functools.partial(forward_kernel, devices), out_shape=(f32...  66.9 us
    pallas_call x1, Pallas kernels, by_longitude(): pl.pallas_call(functools.partial(adjoint_kernel, devices), out_shape=f32(...  47.3 us
    pallas_call x1, Pallas kernels, by_longitude(): pl.pallas_call(functools.partial(share_kernel, devices, slots, foot), out...  22.5 us
    pallas_call x1, Pallas kernels, by_longitude(): pl.pallas_call(functools.partial(scatter_kernel, devices, slots, foot), o...  11.8 us
    pallas_call x1, Pallas kernels, by_longitude(): pl.pallas_call(functools.partial(misfit_kernel, devices), out_shape=f32(d...  8.14 us
    sort x2, local copies, waits for them, and re-layouts, by_longitude(): ordered = lax.sort(jnp.stack([by_lon, by_lat]), dimension=1)  6.94 us

profile of v2, /device:TPU:0, one launch (start us, length us, event | category | flops | bytes accessed | tf_op | source)
XLA Modules:
  0.0 188.3 jit_solution(11110776141440682163)
XLA Ops:
  7.2 0.0 sort.9.cloned.1.call-start
  7.2 0.7 broadcast_multiply_fusion.1
  7.9 0.1 copy.18
  8.0 0.1 mul.96
  8.1 0.8 copy.17
  8.9 0.1 reshape.284
  9.0 0.1 copy.19
  9.1 0.1 mul.102
  9.2 0.1 iota_add_fusion
  9.3 0.6 pad_add_fusion
  9.9 0.0 sort.9.cloned.1.call-update
  10.0 6.9 %sort.9.cloned.1.call-done = s32[2,1024]{1,0:T(2,128)} async-done(((s32[2,1024]{1,0:T(2,128)}), s32[2,1024]{1,0:T(2,128)}) %sort.9.cloned.1.call-update) | async-done | bytes 8208 | tf_op jit(solution)/shard_map/sort | solution.py:686
  16.9 0.9 convert_reduce_fusion
  17.8 0.7 add_add_fusion
  18.5 0.6 reshape.285.list_ref
  19.1 66.9 %shard_map.131 = (f32[4096,128]{1,0:T(8,128)}, f32[128,128]{1,0:T(8,128)}, f32[8,128]{1,0:T(8,128)}, bf16[16,1024,128]{2,1,0:T(8,128)(2,1)}, s32[16,24,128]{2,1,...) custom-call(bf16[1024,128]{1,0:T(8,128)(2,1)} %bitcast.17, s32[24,128]{1,0:T(8,128)} %reshape.285.list_ref, ...), custom_call_target="tpu_custom_call" | custom-call | tf_op jit(solution)/shard_map/pallas_call | solution.py:701
  86.1 1.2 slice_bitcast_fusion.mean
  87.3 22.5 %shard_map.132.part_ref = f32[16,128]{1,0:T(8,128)} custom-call(s32[49152]{0:T(1024)} %bitcast.15, f32[128]{0:T(128)} %slice_bitcast_fusion.mean, bf16[16,1024,128]{2,1,0:T(8,128)(2,1)} %get-tuple-element.11.weights_ref, f32[4096,128]{1,0:T(8,128)} %get-tuple-element.12.inc_ref, f32[256,2048]{1,0:T(8,128)} %bitcast.14, f32[8,2048]{1,0:T(8,128)} %area_ref.3), custom_call_target="tpu_custom_call" | custom-call | tf_op jit(solution)/shard_map/pallas_call | solution.py:727
  109.8 8.1 %shard_map.133 = f32[16,128]{1,0:T(8,128)} custom-call(f32[16,128]{1,0:T(8,128)} %shard_map.132.part_ref, f32[16,128]{1,0:T(8,128)} %get-tuple-element.13.seen_ref, f32[16,128]{1,0:T(8,128)} %get-tuple-element.14.variance_ref), custom_call_target="tpu_custom_call" | custom-call | tf_op jit(solution)/shard_map/pallas_call | solution.py:741
  118.0 11.8 %shard_map.134.grad_ref = f32[4096,128]{1,0:T(8,128)} custom-call(s32[49152]{0:T(1024)} %bitcast.16, f32[2048]{0:T(1024)} %bitcast.18, bf16[16,1024,128]{2,1,0:T(8,128)(2,1)} %get-tuple-element.11.weights_ref), custom_call_target="tpu_custom_call" | custom-call | tf_op jit(solution)/shard_map/pallas_call | solution.py:750
  129.7 0.0 copy-start
  129.7 47.3 %shard_map.135 = f32[256,2048]{1,0:T(8,128)} custom-call(f32[4096,128]{1,0:T(8,128)} %shard_map.134.grad_ref, f32[128,128]{1,0:T(8,128)} %get-tuple-element.15.area_ref, f32[8,128]{1,0:T(8,128)} %get-tuple-element.10.totals_ref, f32[32,32]{1,0:T(8,128)} %time_ref.3, f32[128,128]{1,0:T(8,128)} %lat_ref.3, f32[16,16]{1,0:T(8,128)} %coarse_ref.3, ...), custom_call_target="tpu_custom_call" | custom-call | tf_op jit(solution)/shard_map/pallas_call | solution.py:759
  177.1 0.0 copy-done
  177.1 3.2 %bitcast_add_fusion = f32[32,8,2048]{2,1,0:T(8,128)} fusion(f32[32,8,2048]{2,1,0:T(8,128)S(1)} %copy-done, f32[256,2048]{1,0:T(8,128)} %shard_map.135), kind=kLoop, calls=%fused_computation | loop fusion | flops 524288 | bytes 6291456 | tf_op jit(solution)/shard_map/add | solution.py:776
  180.3 1.2 dynamic-slice_bitcast_fusion
  (4 shorter events, 0.1 us)
Async XLA Ops:
  7.2 9.7 %sort.9.cloned.1.call-start = ((), (), s32[]{:S(2)}) async-start(), calls=%async_computation | async-start | bytes 24608 | tf_op jit(solution)/shard_map/sort | solution.py:686
  129.7 47.3 %copy-start = (f32[32,8,2048]{2,1,0:T(8,128)S(1)}, f32[32,8,2048]{2,1,0:T(8,128)}, u32[]{:S(2)}) copy-start(f32[32,8,2048]{2,1,0:T(8,128)} %param.12) | copy-start | bytes 6291460
Sparse Core Ops, SparseCore 0:
  11.0 5.5 sort.11.cloned.1.call-done
  (1 shorter events, 0.0 us)

commit v3 on v2

--- a/solution.py
+++ b/solution.py
@@ -196,9 +196,12 @@
 
 
 def decode(coded, steps, chunk, first):
-    rows = coded.shape[0]
-    pick = (iota((rows, LANES), 1) == (iota((rows, LANES), 0) + first) // chunk).astype(jnp.float32)
-    return coded.astype(jnp.int32).astype(jnp.float32) * dot(pick, jnp.broadcast_to(steps, (LANES, LANES)), 1, 1)
+    values = coded.astype(jnp.int32).astype(jnp.float32)
+    parts = []
+    for at in range(0, coded.shape[0], chunk):
+        column = (first + at) // chunk
+        parts.append(values[at:at + chunk] * steps[:, column:column + 1])
+    return jnp.concatenate(parts, axis=0)
 
 
 def split(value, size):
@@ -382,7 +385,6 @@
     list_in[me] = list_ref[...]
     for hops in range(2, travel.steps):
         travel.arrive(hops)
-    travel.second()
     for copy in copies:
         copy.wait()
     list_out[...] = list_in[...]
@@ -412,6 +414,8 @@
         for p in range(devices):
             work[p, part] = decode(recvb[p, part], small_in[p, 2 * SUB - 1:2 * SUB], chunk, first)
         lax.fori_loop(half * (hours // 2), (half + 1) * (hours // 2), lat_step, 0, unroll=4)
+        if half == 0:
+            travel.second()
     travel.finish()
 
 

time: 188 us -> 179 us (0.952)
  Pallas kernels: 157 us -> 147 us
    pallas_call x1, Pallas kernels: 66.9 us -> 62.1 us  [by_longitude(): pl.pallas_call(functools.partial(forward_kernel, devices), out_shape=(f32...]
    pallas_call x1, Pallas kernels: 47.3 us -> 44 us  [by_longitude(): pl.pallas_call(functools.partial(adjoint_kernel, devices), out_shape=f32(...]
where the time goes in v3:
time: 179 us; the launch traced here: 178 us
  Pallas kernels  147 us (82%)
  between operations  14.1 us (8%)
  local copies, waits for them, and re-layouts  11.2 us (6%)
  other arithmetic  6.3 us (4%)
    pallas_call x1, Pallas kernels, by_longitude(): pl.pallas_call(functools.partial(forward_kernel, devices), out_shape=(f32...  62.1 us
    pallas_call x1, Pallas kernels, by_longitude(): pl.pallas_call(functools.partial(adjoint_kernel, devices), out_shape=f32(...  44 us
    pallas_call x1, Pallas kernels, by_longitude(): pl.pallas_call(functools.partial(share_kernel, devices, slots, foot), out...  20.9 us
    pallas_call x1, Pallas kernels, by_longitude(): pl.pallas_call(functools.partial(scatter_kernel, devices, slots, foot), o...  11.5 us
    pallas_call x1, Pallas kernels, by_longitude(): pl.pallas_call(functools.partial(misfit_kernel, devices), out_shape=f32(d...  8.35 us
    sort x2, local copies, waits for them, and re-layouts, by_longitude(): ordered = lax.sort(jnp.stack([by_lon, by_lat]), dimension=1)  6.94 us

profile of v3, /device:TPU:0, one launch (start us, length us, event | category | flops | bytes accessed | tf_op | source)
XLA Modules:
  0.0 178.5 jit_solution(175041863657089903)
XLA Ops:
  7.2 0.0 sort.9.cloned.1.call-start
  7.2 0.7 broadcast_multiply_fusion.1
  7.9 0.1 copy.18
  8.0 0.1 mul.96
  8.1 0.8 copy.17
  8.9 0.1 reshape.284
  9.0 0.1 copy.19
  9.1 0.1 mul.102
  9.2 0.1 iota_add_fusion
  9.3 0.6 pad_add_fusion
  9.9 0.0 sort.9.cloned.1.call-update
  10.0 6.9 %sort.9.cloned.1.call-done = s32[2,1024]{1,0:T(2,128)} async-done(((s32[2,1024]{1,0:T(2,128)}), s32[2,1024]{1,0:T(2,128)}) %sort.9.cloned.1.call-update) | async-done | bytes 8208 | tf_op jit(solution)/shard_map/sort | solution.py:690
  16.9 0.9 convert_reduce_fusion
  17.8 0.7 add_add_fusion
  18.5 0.6 reshape.285.list_ref
  19.1 62.1 %shard_map.131 = (f32[4096,128]{1,0:T(8,128)}, f32[128,128]{1,0:T(8,128)}, f32[8,128]{1,0:T(8,128)}, bf16[16,1024,128]{2,1,0:T(8,128)(2,1)}, s32[16,24,128]{2,1,...) custom-call(bf16[1024,128]{1,0:T(8,128)(2,1)} %bitcast.17, s32[24,128]{1,0:T(8,128)} %reshape.285.list_ref, ...), custom_call_target="tpu_custom_call" | custom-call | tf_op jit(solution)/shard_map/pallas_call | solution.py:705
  81.2 1.2 slice_bitcast_fusion.mean
  82.4 20.9 %shard_map.132.part_ref = f32[16,128]{1,0:T(8,128)} custom-call(s32[49152]{0:T(1024)} %bitcast.15, f32[128]{0:T(128)} %slice_bitcast_fusion.mean, bf16[16,1024,128]{2,1,0:T(8,128)(2,1)} %get-tuple-element.11.weights_ref, f32[4096,128]{1,0:T(8,128)} %get-tuple-element.12.inc_ref, f32[256,2048]{1,0:T(8,128)} %bitcast.14, f32[8,2048]{1,0:T(8,128)} %area_ref.3), custom_call_target="tpu_custom_call" | custom-call | tf_op jit(solution)/shard_map/pallas_call | solution.py:731
  103.3 8.3 %shard_map.133 = f32[16,128]{1,0:T(8,128)} custom-call(f32[16,128]{1,0:T(8,128)} %shard_map.132.part_ref, f32[16,128]{1,0:T(8,128)} %get-tuple-element.13.seen_ref, f32[16,128]{1,0:T(8,128)} %get-tuple-element.14.variance_ref), custom_call_target="tpu_custom_call" | custom-call | tf_op jit(solution)/shard_map/pallas_call | solution.py:745
  111.7 11.5 %shard_map.134.grad_ref = f32[4096,128]{1,0:T(8,128)} custom-call(s32[49152]{0:T(1024)} %bitcast.16, f32[2048]{0:T(1024)} %bitcast.18, bf16[16,1024,128]{2,1,0:T(8,128)(2,1)} %get-tuple-element.11.weights_ref), custom_call_target="tpu_custom_call" | custom-call | tf_op jit(solution)/shard_map/pallas_call | solution.py:754
  123.2 0.0 copy-start
  123.2 44.0 %shard_map.135 = f32[256,2048]{1,0:T(8,128)} custom-call(f32[4096,128]{1,0:T(8,128)} %shard_map.134.grad_ref, f32[128,128]{1,0:T(8,128)} %get-tuple-element.15.area_ref, f32[8,128]{1,0:T(8,128)} %get-tuple-element.10.totals_ref, f32[32,32]{1,0:T(8,128)} %time_ref.3, f32[128,128]{1,0:T(8,128)} %lat_ref.3, f32[16,16]{1,0:T(8,128)} %coarse_ref.3, ...), custom_call_target="tpu_custom_call" | custom-call | tf_op jit(solution)/shard_map/pallas_call | solution.py:763
  167.2 0.0 copy-done
  167.2 3.2 %bitcast_add_fusion = f32[32,8,2048]{2,1,0:T(8,128)} fusion(f32[32,8,2048]{2,1,0:T(8,128)S(1)} %copy-done, f32[256,2048]{1,0:T(8,128)} %shard_map.135), kind=kLoop, calls=%fused_computation | loop fusion | flops 524288 | bytes 6291456 | tf_op jit(solution)/shard_map/add | solution.py:780
  170.5 1.2 dynamic-slice_bitcast_fusion
  (4 shorter events, 0.1 us)
Async XLA Ops:
  7.2 9.7 %sort.9.cloned.1.call-start = ((), (), s32[]{:S(2)}) async-start(), calls=%async_computation | async-start | bytes 24608 | tf_op jit(solution)/shard_map/sort | solution.py:690
  123.2 44.0 %copy-start = (f32[32,8,2048]{2,1,0:T(8,128)S(1)}, f32[32,8,2048]{2,1,0:T(8,128)}, u32[]{:S(2)}) copy-start(f32[32,8,2048]{2,1,0:T(8,128)} %param.12) | copy-start | bytes 6291460
Sparse Core Ops, SparseCore 0:
  11.0 5.5 sort.11.cloned.1.call-done
  (1 shorter events, 0.0 us)
